TPU v7x, 256 devices: a whole 4x4x8 slice. The times are simulated.
256 devices in a mesh: region: 16 (over x, y), within: 16 (over z, core).
Axes of the slice: x: 4, y: 4, z: 8, core: 2. Of those that a mesh axis runs over, the one named last changes fastest.
Arguments:
- kernel_tiles: bfloat16 [8192, 5, 128, 128], P(('region', 'within')), as said below
- neighbours: int32 [8192, 5], P(('region', 'within')), may hold values from 0 to 8191, as said below
- tile_counts: int32 [8192], P(('region', 'within')), may hold values from 1 to 5, as said below
- start_block: float32 [1048576, 64], P(('region', 'within'))
Outputs:
- last_block: float32 [1048576, 64], P(('region', 'within'))
- hessenberg: float32 [320, 256], replicated
Inputs may be any that keep to these rules, and one draw needn't show every extreme that they name: `neighbours`: slot 0 of every milestone names the milestone itself; the live slots of a milestone name distinct milestones at most 2 away from it; slots that are not live name the milestone itself. `tile_counts`: some milestone has all 5 slots live. `kernel_tiles`: all entries are positive.
All inputs are finite; a program needn't handle non-finite values.
Results may differ from a plain program's by a relative error of at most 0.0075.
Values may be sent and summed in bfloat16 or wider, within the bound.
A program may use at most 64 MiB of HBM per device.

v0:
```python
import jax
import jax.numpy as jnp
from jax import lax
from jax.sharding import PartitionSpec as P

REACH = 2
STEPS = 4


def with_halo(value, sides, width):
    for axis, dim in sides:
        count, length = (lax.axis_size(axis), value.shape[dim])
        up = [(i, (i + 1) % count) for i in range(count - 1)]
        down = [(j, i) for i, j in up]
        last = lax.slice_in_dim(value, length - width, length, axis=dim)
        initial = lax.slice_in_dim(value, 0, width, axis=dim)
        before = lax.ppermute(last, axis, up)
        after = lax.ppermute(initial, axis, down)
        value = jnp.concatenate([before, value, after], axis=dim)
    return value


def finish_orth(block, chol_lower):
    identity = jnp.eye(block.shape[1], dtype=jnp.float32)
    inverse = jax.scipy.linalg.solve_triangular(chol_lower, identity, lower=True)
    return (jnp.dot(block, inverse.T, precision=lax.Precision.HIGHEST), chol_lower.T)


def orthonormal(block, inv_rows):
    local_gram = jnp.einsum("rc,rd->cd", block, block, precision=lax.Precision.HIGHEST)
    gram = lax.psum(local_gram, ("region", "within"))
    chol_lower = jnp.linalg.cholesky(gram * inv_rows)
    return finish_orth(block, chol_lower)


def tile_product(slot_index, tile_part, live_part, source_rows):
    gathered = jnp.where(
        live_part[:, :, None, None], source_rows[slot_index], jnp.zeros((), jnp.bfloat16)
    )
    return jnp.einsum("mkab,mkbc->mac", tile_part, gathered, preferred_element_type=jnp.float32)


def on_device(kernel_tiles, neighbours, tile_counts, start_block):
    row_count, block_width = start_block.shape
    milestones, slot_count, state_count = (
        kernel_tiles.shape[0],
        kernel_tiles.shape[1],
        kernel_tiles.shape[2],
    )
    reach_ms = REACH
    inv_rows = 1.0 / (row_count * lax.axis_size("region") * lax.axis_size("within"))
    slot_ids = jnp.arange(slot_count, dtype=jnp.int32)
    live_slots = slot_ids[None, :] < tile_counts[:, None]
    live_ones = jnp.broadcast_to(
        live_slots.astype(jnp.bfloat16)[:, :, None], (milestones, slot_count, state_count)
    )
    row_sums = jnp.einsum(
        "mkab,mkb->ma", kernel_tiles, live_ones, preferred_element_type=jnp.float32
    )
    first_id = neighbours[0, 0]
    local_index = neighbours - first_id
    first_block, unused_factor = orthonormal(start_block, inv_rows)
    krylov_basis = [first_block]
    hessenberg = jnp.zeros(((STEPS + 1) * block_width, STEPS * block_width), jnp.float32)
    for number in range(STEPS):
        shaped = krylov_basis[-1].astype(jnp.bfloat16).reshape(milestones, state_count, block_width)
        extended = with_halo(shaped, ((("region", "within"), 0),), reach_ms)
        product_rows = tile_product(local_index + reach_ms, kernel_tiles, live_slots, extended)
        image = (product_rows / row_sums[:, :, None]).reshape(row_count, block_width)
        stacked = jnp.concatenate(krylov_basis, axis=1)
        local_inner = jnp.einsum("rc,rd->cd", stacked, image, precision=lax.Precision.HIGHEST)
        projected = lax.psum(local_inner, ("region", "within")) * inv_rows
        remainder = image - jnp.dot(stacked, projected, precision=lax.Precision.HIGHEST)
        next_block, factor = orthonormal(remainder, inv_rows)
        hessenberg = hessenberg.at[
            : (number + 1) * block_width, number * block_width : (number + 1) * block_width
        ].set(projected)
        hessenberg = hessenberg.at[
            (number + 1) * block_width : (number + 2) * block_width,
            number * block_width : (number + 1) * block_width,
        ].set(factor)
        krylov_basis.append(next_block)
    return (krylov_basis[-1], hessenberg)


def solution(mesh):
    return jax.shard_map(
        on_device,
        mesh=mesh,
        in_specs=(
            P(("region", "within"), None, None, None),
            P(("region", "within"), None),
            P(("region", "within")),
            P(("region", "within"), None),
        ),
        out_specs=(P(("region", "within"), None), P()),
        check_vma=False,
    )
```

profile of v0, /device:TPU:8, one launch (start us, length us, event | category | flops | bytes accessed | tf_op | source)
XLA Modules:
  0.0 1060.7 jit_solution(15112724343179177714)
XLA Ops:
  9.4 78.7 %psum.63 = f32[64,64]{0,1:T(8,128)S(1)} all-reduce(f32[64,64]{0,1:T(8,128)S(1)} %fusion.100), channel_id=1, replica_groups=mesh['region'=16,'within'=16] {'region','within'}, use_global_device_ids=true, to_apply=%region_0.0 | all-reduce | flops 4096 | bytes 32768 | tf_op jit(solution)/shard_map/psum | solution.py:31
  88.2 5.8 cholesky.89
  95.4 4.9 custom-call.9
  120.2 5.6 divide_bitcast_fusion.3
  127.7 77.3 %psum.64 = f32[64,64]{0,1:T(8,128)S(1)} all-reduce(f32[64,64]{0,1:T(8,128)S(1)} %fusion.34), channel_id=1, replica_groups=mesh['region'=16,'within'=16] {'region','within'}, use_global_device_ids=true, to_apply=%region_3.6 | all-reduce | flops 4096 | bytes 32768 | tf_op jit(solution)/shard_map/psum | solution.py:72
  208.3 73.5 %psum.65 = f32[64,64]{0,1:T(8,128)S(1)} all-reduce(f32[64,64]{0,1:T(8,128)S(1)} %fusion.101), channel_id=1, replica_groups=mesh['region'=16,'within'=16] {'region','within'}, use_global_device_ids=true, to_apply=%region_4.7 | all-reduce | flops 4096 | bytes 32768 | tf_op jit(solution)/shard_map/psum | solution.py:31
  281.9 5.8 cholesky.100
  289.7 4.9 custom-call.10
  312.6 5.7 divide_bitcast_fusion.2
  322.2 75.7 %psum.66 = f32[128,64]{0,1:T(8,128)} all-reduce(f32[128,64]{0,1:T(8,128)} %fusion.14), channel_id=1, replica_groups=mesh['region'=16,'within'=16] {'region','within'}, use_global_device_ids=true, to_apply=%region_5.8 | all-reduce | flops 8192 | bytes 65536 | tf_op jit(solution)/shard_map/psum | solution.py:72
  402.5 73.5 %psum.67 = f32[64,64]{0,1:T(8,128)S(1)} all-reduce(f32[64,64]{0,1:T(8,128)S(1)} %fusion.102), channel_id=1, replica_groups=mesh['region'=16,'within'=16] {'region','within'}, use_global_device_ids=true, to_apply=%region_6.9 | all-reduce | flops 4096 | bytes 32768 | tf_op jit(solution)/shard_map/psum | solution.py:31
  476.1 5.8 cholesky.111
  483.3 4.9 custom-call.11
  508.2 5.8 divide_bitcast_fusion.1
  518.7 77.9 %psum.68 = f32[192,64]{0,1:T(8,128)} all-reduce(f32[192,64]{0,1:T(8,128)} %fusion.13), channel_id=1, replica_groups=mesh['region'=16,'within'=16] {'region','within'}, use_global_device_ids=true, to_apply=%region_7.10 | all-reduce | flops 12288 | bytes 98304 | tf_op jit(solution)/shard_map/psum | solution.py:72
  602.4 74.1 %psum.69 = f32[64,64]{0,1:T(8,128)S(1)} all-reduce(f32[64,64]{0,1:T(8,128)S(1)} %fusion.103), channel_id=1, replica_groups=mesh['region'=16,'within'=16] {'region','within'}, use_global_device_ids=true, to_apply=%region_8.11 | all-reduce | flops 4096 | bytes 32768 | tf_op jit(solution)/shard_map/psum | solution.py:31
  676.6 5.8 cholesky.122
  684.3 4.9 custom-call.12
  698.4 5.0 collective-permute-done.6
  706.1 5.7 divide_bitcast_fusion
  726.9 224.1 %all-reduce.3.cloned.1.call-done = f32[256,64]{0,1:T(8,128)} async-done(((f32[256,64]{0,1:T(8,128)}), f32[256,64]{0,1:T(8,128)}) %all-reduce.3.cloned.1.call-update) | async-done | bytes 65552 | tf_op jit(solution)/shard_map/psum | solution.py:72
  957.6 74.5 %psum.71 = f32[64,64]{0,1:T(8,128)S(1)} all-reduce(f32[64,64]{0,1:T(8,128)S(1)} %fusion.104), channel_id=1, replica_groups=mesh['region'=16,'within'=16] {'region','within'}, use_global_device_ids=true, to_apply=%region_10.13 | all-reduce | flops 4096 | bytes 32768 | tf_op jit(solution)/shard_map/psum | solution.py:31
  1032.2 5.8 cholesky.133
  1039.4 4.9 custom-call.13
  (165 shorter events, 134.7 us)
Async XLA Ops:
  7.2 1.3 copy-start
  7.2 103.4 %copy-start.19 = (s32[2]{0:T(128)S(1)}, s32[2]{0:T(128)}, u32[]{:S(2)}) copy-start(s32[2]{0:T(128)} %constant.244.clone.1) | copy-start | bytes 28
  7.2 104.7 %copy-start.18 = (s32[2]{0:T(128)S(1)}, s32[2]{0:T(128)}, u32[]{:S(2)}) copy-start(s32[2]{0:T(128)} %constant.245.clone.1) | copy-start | bytes 28
  7.2 100.7 %copy-start.15 = (s32[32,5]{0,1:T(8,128)S(1)}, s32[32,5]{0,1:T(8,128)}, u32[]{:S(2)}) copy-start(s32[32,5]{0,1:T(8,128)} %param.24) | copy-start | bytes 1924
  7.2 102.1 %copy-start.16 = (s32[32]{0:T(128)S(1)}, s32[32]{0:T(128)}, u32[]{:S(2)}) copy-start(s32[32]{0:T(128)} %param.25) | copy-start | bytes 388
  7.2 943.7 %all-reduce.3.cloned.1.call-start = ((), (), s32[]{:S(2)}) async-start(), calls=%async_computation | async-start | bytes 131072 | tf_op jit(solution)/shard_map/psum | solution.py:72
  101.6 15.9 %collective-permute-start.1 = (bf16[2,128,64]{1,2,0:T(8,128)(2,1)S(1)}, bf16[2,128,64]{1,2,0:T(8,128)(2,1)S(1)}, u32[]{:S(2)}, u32[]{:S(2)}) collective-permute-start(bf16[2,128,64]{1,2,0:T(8,128)(2,1)S(1)} %bitcast.214), channel_id=1, source_target_pairs={{1,0},{2,1},{3,2},{4,3},{5,4},{6,5},{7,6},{8,7},{9,8},{10,9},{11,1... | collective-permute-start | bytes 98312 | tf_op jit(solution)/shard_map/ppermute | solution.py:18
  105.8 11.7 %collective-permute-start = (bf16[2,128,64]{1,2,0:T(8,128)(2,1)S(1)}, bf16[2,128,64]{1,2,0:T(8,128)(2,1)S(1)}, u32[]{:S(2)}, u32[]{:S(2)}) collective-permute-start(bf16[2,128,64]{1,2,0:T(8,128)(2,1)S(1)} %bitcast.215), channel_id=1, source_target_pairs={{0,1},{1,2},{2,3},{3,4},{4,5},{5,6},{6,7},{7,8},{8,9},{9,10},{10,1... | collective-permute-start | bytes 98312 | tf_op jit(solution)/shard_map/ppermute | solution.py:17
  116.8 3.4 copy-start.17
  297.9 8.1 collective-permute-start.3
  301.6 7.3 collective-permute-start.2
  312.6 6.7 copy-start.1
  401.5 97.5 %copy-start.13 = (f32[128,64]{0,1:T(8,128)S(1)}, f32[128,64]{0,1:T(8,128)}, u32[]{:S(2)}) copy-start(f32[128,64]{0,1:T(8,128)} %psum.66) | copy-start | bytes 98308
  492.7 11.8 %collective-permute-start.5 = (bf16[2,128,64]{1,2,0:T(8,128)(2,1)S(1)}, bf16[2,128,64]{1,2,0:T(8,128)(2,1)S(1)}, u32[]{:S(2)}, u32[]{:S(2)}) collective-permute-start(bf16[2,128,64]{1,2,0:T(8,128)(2,1)S(1)} %bitcast.216), channel_id=1, source_target_pairs={{1,0},{2,1},{3,2},{4,3},{5,4},{6,5},{7,6},{8,7},{9,8},{10,9},{11,1... | collective-permute-start | bytes 98312 | tf_op jit(solution)/shard_map/ppermute | solution.py:18
  497.0 7.6 collective-permute-start.4
  508.2 6.8 copy-start.2
  508.2 6.8 copy-start.9
  692.7 5.7 collective-permute-start.7
  696.1 7.3 collective-permute-start.6
  706.1 6.7 copy-start.3
  706.1 6.7 copy-start.10
  706.1 6.7 copy-start.11
  955.6 1.0 copy-start.6
  956.6 91.2 %copy-start.14 = (f32[256,64]{0,1:T(8,128)S(1)}, f32[256,64]{0,1:T(8,128)}, u32[]{:S(2)}) copy-start(f32[256,64]{0,1:T(8,128)} %all-reduce.3.cloned.1.call-done) | copy-start | bytes 196612
  (6 other events, 5.9 us)
Sparse Core Ops, SparseCore 0:
  717.6 233.3 all-reduce.2
where the time goes:
time: 1070 us; the launch traced here: 1060 us
  blocking collectives  605 us (57%)
  waiting for transfers between devices  232 us (22%)
  other arithmetic  74.8 us (7%)
  matrix products  71.5 us (7%)
  local copies, waits for them, and re-layouts  38.2 us (4%)
  starting transfers between devices  23.7 us (2%)
  between operations  15.2 us (1%)
    psum x5, blocking collectives, orthonormal(): gram = lax.psum(local_gram, ('region', 'within'))  374 us
    psum x3, blocking collectives, on_device(): projected = lax.psum(local_inner, ('region', 'within')) * inv_rows  231 us
    psum x1, waiting for transfers between devices, on_device(): projected = lax.psum(local_inner, ('region', 'within')) * inv_rows  224 us
    another operation x15, other arithmetic, orthonormal(): chol_lower = jnp.linalg.cholesky(gram * inv_rows)  32.6 us
    another operation x7, other arithmetic, finish_orth(): jax.scipy.linalg.solve_triangular(chol_lower, identity, lower=True)  25.8 us
    dot_general x4, matrix products, tile_product(): jnp.einsum('mkab,mkbc->mac', tile_part, gathered, preferred_element_type=...  22.8 us
  transfers between devices with their start and end apart: 9, of which 3 were waited for; matrix products, arithmetic and copies ran while one was open for 3% of the time, Pallas kernels for 0%

commit v1 on v0

v1 whole, which is shorter than its diff:
```python
import functools

import jax
import jax.numpy as jnp
from jax import lax
from jax.experimental import pallas as pl
from jax.experimental.pallas import tpu as pltpu
from jax.sharding import PartitionSpec as P

REACH = 2
STEPS = 4
NBLK = STEPS + 1
SHIFTS = (0.0, 0.5, 1.0, 0.25)
F32 = jnp.float32
BF16 = jnp.bfloat16
MESH = pl.DeviceIdType.MESH
HIGHEST = lax.Precision.HIGHEST
NT = (((1,), (1,)), ((), ()))
TN = (((0,), (0,)), ((), ()))
NN = (((1,), (0,)), ((), ()))
ROWS_A, ROWS_B = 384, 256
BATCHES = ((0, ROWS_A), (ROWS_A, ROWS_B))


def place(i, j):
    if j < STEPS:
        t = j * (j + 1) // 2 + i
        return (t // 2) * 64, t % 2
    return ROWS_A + (i // 2) * 64, i % 2


def split(x):
    hi = x.astype(BF16)
    lo = (x - hi.astype(F32)).astype(BF16)
    return jnp.concatenate([hi, lo], axis=0)


def krylov_kernel(
    nr, nw, nbr, cnt, tiles, start, s_out, z_out,
    tl, x0, vb, ones, irs, hb, acc, gb, land1, part, land2, gs,
    in_sem, z_sem, hs, hr, s1, r1, s2, r2, s3, r3,
):
    mil = tl.shape[0]
    slots = tl.shape[1]
    zero_at = mil + 2 * REACH
    n = nr * nw
    me_r = lax.axis_index("region")
    me_w = lax.axis_index("within")
    me = me_r * nw + me_w
    base = me * mil
    right = lax.rem(me + 1, n)
    left = lax.rem(me + n - 1, n)
    right_id = (right // nw, lax.rem(right, nw))
    left_id = (left // nw, lax.rem(left, nw))

    start_copy = pltpu.make_async_copy(start, x0, in_sem.at[0])
    start_copy.start()
    part_mil = mil // 4
    tile_copies = []
    for c in range(4):
        cp = pltpu.make_async_copy(
            tiles.at[pl.ds(c * part_mil, part_mil)],
            tl.at[pl.ds(c * part_mil, part_mil)],
            in_sem.at[1 + c],
        )
        cp.start()
        tile_copies.append(cp)

    barrier = pltpu.get_barrier_semaphore()
    for o in range(1, nr):
        pl.semaphore_signal(
            barrier, inc=1, device_id=(lax.rem(me_r + o, nr), me_w), device_id_type=MESH
        )
    for o in range(1, nw):
        pl.semaphore_signal(
            barrier, inc=1, device_id=(me_r, lax.rem(me_w + o, nw)), device_id_type=MESH
        )
    pl.semaphore_signal(barrier, inc=1, device_id=right_id, device_id_type=MESH)
    pl.semaphore_signal(barrier, inc=1, device_id=left_id, device_id_type=MESH)

    for j in range(STEPS):
        vb[j, zero_at] = jnp.zeros((128, 128), BF16)
    ones[0] = jnp.ones((16, 128), BF16)
    ones[1] = jnp.zeros((16, 128), BF16)
    gb[ROWS_A - 64 : ROWS_A] = jnp.zeros((64, 128), F32)
    gb[ROWS_A + ROWS_B - 64 :] = jnp.zeros((64, 128), F32)

    start_copy.wait()

    def load_start(m):
        lanes = pl.ds(pl.multiple_of(m * 128, 128), 128)
        vb[0, m + REACH] = split(x0[:, lanes])

    edge = list(range(REACH)) + list(range(mil - REACH, mil))
    for m in edge:
        load_start(m)
    pl.semaphore_wait(barrier, nr + nw)

    def halo(j):
        return (
            pltpu.make_async_remote_copy(
                src_ref=vb.at[j, pl.ds(mil, REACH)], dst_ref=hb.at[j, 0],
                send_sem=hs.at[j, 0], recv_sem=hr.at[j, 0],
                device_id=right_id, device_id_type=MESH,
            ),
            pltpu.make_async_remote_copy(
                src_ref=vb.at[j, pl.ds(REACH, REACH)], dst_ref=hb.at[j, 1],
                send_sem=hs.at[j, 1], recv_sem=hr.at[j, 1],
                device_id=left_id, device_id_type=MESH,
            ),
        )

    def start_all(copies):
        for cp in copies:
            cp.start()

    def apply_one(j, m):
        vs, ts = [], []
        for k in range(slots):
            live = k < cnt[m]
            at = jnp.where(live, nbr[k, m] - base + REACH, zero_at)
            v = vb[j, at]
            if j == 0:
                v = jnp.concatenate([v, ones[jnp.where(live, 0, 1)]], axis=0)
            vs.append(v)
            ts.append(tl[m, k])
        prod = lax.dot_general(
            jnp.concatenate(vs, axis=1), jnp.concatenate(ts, axis=1), NT,
            preferred_element_type=F32,
        )
        if j == 0:
            inv = 1.0 / prod[128:136]
            irs[m] = inv
        else:
            inv = irs[m]
        w = (prod[:64] + prod[64:128]) * inv[0:1]
        if SHIFTS[j] != 0.0:
            own = vb[j, m + REACH].astype(F32)
            w = w - SHIFTS[j] * (own[:64] + own[64:])
        vb[j + 1, m + REACH] = split(w)

    group = 8

    def gram(j):
        rows = (j + 1) * 128

        def body(c, carry):
            stack = []
            for i in range(j + 1):
                stack.append(
                    jnp.concatenate(
                        [vb[i, REACH + c * group + q] for q in range(group)], axis=1
                    )
                )
            prod = lax.dot_general(
                jnp.concatenate(stack, axis=0), stack[j], NT, preferred_element_type=F32
            )

            @pl.when(c == 0)
            def _():
                acc[:rows] = prod

            @pl.when(c > 0)
            def _():
                acc[:rows] += prod

            return carry

        lax.fori_loop(0, mil // group, body, 0)
        lane = lax.broadcasted_iota(jnp.int32, (64, 128), 1)
        for i in range(j + 1):
            blk = acc[i * 128 : i * 128 + 64] + acc[i * 128 + 64 : i * 128 + 128]
            blk = blk + pltpu.roll(blk, 64, 1)
            row, odd = place(i, j)
            if odd:
                gb[row : row + 64] = jnp.where(lane < 64, gb[row : row + 64], blk)
            else:
                gb[row : row + 64] = blk

    def rows_of(b, c):
        first, total = BATCHES[b]
        size = total // nr
        return pl.ds(pl.multiple_of(first + c * size, 8), size)

    def stage1(b):
        size = BATCHES[b][1] // nr
        out = []
        for o in range(1, nr):
            to = lax.rem(me_r + o, nr)
            out.append(
                pltpu.make_async_remote_copy(
                    src_ref=gb.at[rows_of(b, to)],
                    dst_ref=land1.at[b, o - 1, pl.ds(0, size)],
                    send_sem=s1.at[b, o - 1], recv_sem=r1.at[b, o - 1],
                    device_id=(to, me_w), device_id_type=MESH,
                )
            )
        return out

    def sum1(b):
        size = BATCHES[b][1] // nr
        total = gb[rows_of(b, me_r)]
        for o in range(1, nr):
            total = total + land1[b, o - 1, 0:size]
        part[b, 0:size] = total
        land2[b, me_w, 0:size] = total

    def stage2(b):
        size = BATCHES[b][1] // nr
        out = []
        for o in range(1, nw):
            to = lax.rem(me_w + o, nw)
            out.append(
                pltpu.make_async_remote_copy(
                    src_ref=part.at[b, pl.ds(0, size)],
                    dst_ref=land2.at[b, me_w, pl.ds(0, size)],
                    send_sem=s2.at[b, o - 1], recv_sem=r2.at[b, o - 1],
                    device_id=(me_r, to), device_id_type=MESH,
                )
            )
        return out

    def wait2(b):
        size = BATCHES[b][1] // nr
        for o in range(1, nw):
            frm = lax.rem(me_w + nw - o, nw)
            pltpu.make_async_remote_copy(
                src_ref=part.at[b, pl.ds(0, size)],
                dst_ref=land2.at[b, frm, pl.ds(0, size)],
                send_sem=s2.at[b, o - 1], recv_sem=r2.at[b, o - 1],
                device_id=(me_r, frm), device_id_type=MESH,
            ).wait_recv()

    def sum2(b):
        size = BATCHES[b][1] // nr
        total = land2[b, 0, 0:size]
        for i in range(1, nw):
            total = total + land2[b, i, 0:size]
        gs[rows_of(b, me_r)] = total

    def stage3(b):
        out = []
        for o in range(1, nr):
            to = lax.rem(me_r + o, nr)
            out.append(
                pltpu.make_async_remote_copy(
                    src_ref=gs.at[rows_of(b, me_r)],
                    dst_ref=gs.at[rows_of(b, me_r)],
                    send_sem=s3.at[b, o - 1], recv_sem=r3.at[b, o - 1],
                    device_id=(to, me_w), device_id_type=MESH,
                )
            )
        return out

    def wait3(b):
        for o in range(1, nr):
            frm = lax.rem(me_r + nr - o, nr)
            pltpu.make_async_remote_copy(
                src_ref=gs.at[rows_of(b, frm)],
                dst_ref=gs.at[rows_of(b, frm)],
                send_sem=s3.at[b, o - 1], recv_sem=r3.at[b, o - 1],
                device_id=(frm, me_w), device_id_type=MESH,
            ).wait_recv()

    def wait_sent(copies):
        for cp in copies:
            cp.wait_send()

    def wait_got(copies):
        for cp in copies:
            cp.wait_recv()

    def interior(fn):
        def body(m, carry):
            fn(m)
            return carry

        lax.fori_loop(REACH, mil - REACH, body, 0, unroll=2)

    halos = [halo(j) for j in range(STEPS)]
    z_copies = [
        pltpu.make_async_copy(vb.at[j, pl.ds(REACH, mil)], z_out.at[j], z_sem.at[j])
        for j in range(NBLK)
    ]
    first = [stage1(b) for b in range(2)]
    second = [stage2(b) for b in range(2)]
    third = [stage3(b) for b in range(2)]

    start_all(halos[0])
    interior(load_start)
    for j in range(STEPS):
        z_copies[j].start()
        gram(j)
        if j == 0:
            for cp in tile_copies:
                cp.wait()
        if j == STEPS - 1:
            start_all(first[0])
        interior(functools.partial(apply_one, j))
        wait_got(halos[j])
        vb[j, 0:REACH] = hb[j, 0]
        vb[j, mil + REACH : mil + 2 * REACH] = hb[j, 1]
        for m in edge:
            apply_one(j, m)
        if j + 1 < STEPS:
            start_all(halos[j + 1])
    z_copies[STEPS].start()
    wait_got(first[0])
    sum1(0)
    start_all(second[0])
    gram(STEPS)
    start_all(first[1])
    wait2(0)
    sum2(0)
    start_all(third[0])
    wait_got(first[1])
    sum1(1)
    start_all(second[1])
    wait3(0)
    wait2(1)
    sum2(1)
    start_all(third[1])
    for j in range(STEPS):
        wait_sent(halos[j])
    for b in range(2):
        wait_sent(first[b])
        wait_sent(second[b])
    wait_sent(third[0])
    for cp in z_copies:
        cp.wait()
    wait3(1)
    s_out[...] = gs[...]
    wait_sent(third[1])


def mm(a, b, dims=NN):
    return lax.dot_general(a, b, dims, precision=HIGHEST, preferred_element_type=F32)


def factor(block):
    size = block.shape[0]
    eye = (
        lax.broadcasted_iota(jnp.int32, (size, size), 0)
        == lax.broadcasted_iota(jnp.int32, (size, size), 1)
    ).astype(F32)
    cur = jnp.concatenate([block, eye], axis=1)
    done = []
    for kb in range(size // 8):
        n = size - 8 * kb
        rid = lax.broadcasted_iota(jnp.int32, (n, 128), 0)
        cols = [
            jnp.broadcast_to(cur[:, 8 * kb + p : 8 * kb + p + 1], (n, 128)) for p in range(8)
        ]
        scale = jnp.zeros((8, 128), F32)
        for p in range(8):
            pivot = cols[p][p : p + 1]
            inv = 1.0 / pivot
            scale = jnp.where(rid[:8] == p, lax.rsqrt(pivot), scale)
            mult = jnp.where(rid > p, cols[p] * inv, 0.0)
            cur = cur - mult * cur[p : p + 1]
            for q in range(p + 1, 8):
                cols[q] = cols[q] - mult * cols[q][p : p + 1]
        done.append(cur[:8] * scale)
        cur = cur[8:]
    full = jnp.concatenate(done, axis=0)
    upper = lax.broadcasted_iota(jnp.int32, (size, size), 0) <= lax.broadcasted_iota(
        jnp.int32, (size, size), 1
    )
    r = jnp.where(upper, full[:, :size], 0.0)
    m = pltpu.roll(full, size, 1)[:, :size]
    return r, m


def finish_kernel(scale, s_ref, z_hbm, q_ref, h_ref, zb, sems):
    mil = zb.shape[1]
    copies = [pltpu.make_async_copy(z_hbm.at[k], zb.at[k], sems.at[k]) for k in range(NBLK)]
    for cp in copies:
        cp.start()

    def gram_block(i, j):
        row, odd = place(i, j)
        x = s_ref[row : row + 64]
        if odd:
            x = pltpu.roll(x, 64, 1)
        return x[:, :64] * scale

    r = [[None] * NBLK for _ in range(NBLK)]
    inv = [[None] * NBLK for _ in range(NBLK)]
    for j in range(NBLK):
        schur = gram_block(j, j)
        if j:
            r_col = None
            for k in range(j):
                stack = jnp.concatenate(
                    [inv[k][i] for i in range(k, j)], axis=0
                )
                term = mm(stack, gram_block(k, j))
                if k:
                    term = jnp.concatenate([jnp.zeros((64 * k, 64), F32), term], axis=0)
                r_col = term if r_col is None else r_col + term
            for i in range(j):
                r[i][j] = r_col[64 * i : 64 * i + 64]
            schur = schur - mm(r_col, r_col, TN)
        r[j][j], inv[j][j] = factor(schur)
        for k in range(j):
            stack = jnp.concatenate([inv[k][i] for i in range(k, j)], axis=0)
            t = mm(r_col[64 * k :], stack, TN)
            inv[k][j] = -mm(inv[j][j], t)

    coef = []
    for k in range(NBLK):
        c = inv[k][STEPS]
        hi = c.astype(BF16)
        lo = (c - hi.astype(F32)).astype(BF16)
        coef.append(
            jnp.concatenate(
                [jnp.concatenate([hi, hi], axis=1), jnp.concatenate([lo, lo], axis=1)], axis=0
            )
        )
    coef = jnp.concatenate(coef, axis=1)

    for j in range(STEPS):
        col = None
        for k in range(j + 1):
            parts = []
            for i in range(k + 2):
                x = r[i][k + 1]
                if i <= k and SHIFTS[k] != 0.0:
                    x = x + SHIFTS[k] * r[i][k]
                parts.append(x)
            term = mm(jnp.concatenate(parts, axis=0), inv[k][j], NT)
            if k < j:
                term = jnp.concatenate([term, jnp.zeros((64 * (j - k), 64), F32)], axis=0)
            col = term if col is None else col + term
        if j + 2 < NBLK:
            col = jnp.concatenate([col, jnp.zeros((64 * (NBLK - j - 2), 64), F32)], axis=0)
        h_ref[:, 64 * j : 64 * j + 64] = col

    for cp in copies:
        cp.wait()

    def body(g, carry):
        m = 2 * g
        right = jnp.concatenate(
            [
                jnp.concatenate([zb[k, m], zb[k, m + 1]], axis=1)
                for k in range(NBLK)
            ],
            axis=0,
        )
        prod = lax.dot_general(coef, right, NN, preferred_element_type=F32)
        q_ref[:, pl.ds(pl.multiple_of(g * 256, 256), 256)] = prod[:64] + prod[64:]
        return carry

    lax.fori_loop(0, mil // 2, body, 0)


def on_device(nr, nw, kernel_tiles, neighbours, tile_counts, start_block):
    mil, slots, states = kernel_tiles.shape[:3]
    width = start_block.shape[1]
    rows = mil * states
    vmem = pl.BlockSpec(memory_space=pltpu.VMEM)
    smem = pl.BlockSpec(memory_space=pltpu.SMEM)
    hbm = pl.BlockSpec(memory_space=pl.ANY)
    size = ROWS_A // nr
    dma = pltpu.SemaphoreType.DMA
    packed, z = pl.pallas_call(
        functools.partial(krylov_kernel, nr, nw),
        out_shape=(
            jax.ShapeDtypeStruct((ROWS_A + ROWS_B, 128), F32),
            jax.ShapeDtypeStruct((NBLK, mil, 2 * width, states), BF16),
        ),
        in_specs=[smem, smem, hbm, hbm],
        out_specs=(vmem, hbm),
        scratch_shapes=[
            pltpu.VMEM((mil, slots, states, states), BF16),
            pltpu.VMEM((width, rows), F32),
            pltpu.VMEM((NBLK, mil + 2 * REACH + 1, 2 * width, states), BF16),
            pltpu.VMEM((2, 16, 128), BF16),
            pltpu.VMEM((mil, 8, 128), F32),
            pltpu.VMEM((STEPS, 2, REACH, 2 * width, states), BF16),
            pltpu.VMEM((NBLK * 128, 128), F32),
            pltpu.VMEM((ROWS_A + ROWS_B, 128), F32),
            pltpu.VMEM((2, nr, size, 128), F32),
            pltpu.VMEM((2, size, 128), F32),
            pltpu.VMEM((2, nw, size, 128), F32),
            pltpu.VMEM((ROWS_A + ROWS_B, 128), F32),
            dma((5,)), dma((NBLK,)),
            dma((STEPS, 2)), dma((STEPS, 2)),
            dma((2, nr)), dma((2, nr)),
            dma((2, nw)), dma((2, nw)),
            dma((2, nr)), dma((2, nr)),
        ],
        compiler_params=pltpu.CompilerParams(
            collective_id=0, has_side_effects=True, vmem_limit_bytes=40 * 1024 * 1024
        ),
    )(neighbours.T, tile_counts, kernel_tiles, start_block.T)
    last, hess = pl.pallas_call(
        functools.partial(finish_kernel, 1.0 / (rows * nr * nw)),
        out_shape=(
            jax.ShapeDtypeStruct((width, rows), F32),
            jax.ShapeDtypeStruct((NBLK * width, STEPS * width), F32),
        ),
        in_specs=[vmem, hbm],
        out_specs=(vmem, vmem),
        scratch_shapes=[
            pltpu.VMEM((NBLK, mil, 2 * width, states), BF16),
            dma((NBLK,)),
        ],
        compiler_params=pltpu.CompilerParams(vmem_limit_bytes=40 * 1024 * 1024),
    )(packed, z)
    return last.T, hess


def solution(mesh):
    nr, nw = mesh.shape["region"], mesh.shape["within"]
    return jax.shard_map(
        functools.partial(on_device, nr, nw),
        mesh=mesh,
        in_specs=(
            P(("region", "within"), None, None, None),
            P(("region", "within"), None),
            P(("region", "within")),
            P(("region", "within"), None),
        ),
        out_specs=(P(("region", "within"), None), P()),
        check_vma=False,
    )
```

time: 1070 us -> 92.6 us (0.09)
  blocking collectives: 605 us -> 0 us
  waiting for transfers between devices: 232 us -> 0 us
  Pallas kernels: 0 us -> 85.8 us
  other arithmetic: 74.8 us -> 0 us
  matrix products: 71.5 us -> 0 us
  local copies, waits for them, and re-layouts: 38.2 us -> 5.04 us
  starting transfers between devices: 23.7 us -> 0 us
  between operations: 15.2 us -> 0.81 us
    psum x8 -> x0, blocking collectives: 605 us -> none  [the longest x5 374 us: orthonormal(): gram = lax.psum(local_gram, ('region', 'within'))]
    psum x1 -> x0, waiting for transfers between devices: 224 us -> none  [on_device(): projected = lax.psum(local_inner, ('region', 'within')) * inv_rows]
    pallas_call x0 -> x2, Pallas kernels: none -> 85.8 us  [the longest x1 66.8 us: on_device(): pl.pallas_call(functools.partial(krylov_kernel, nr, nw), out_shape=(jax.S...]
    another operation x34 -> x0, other arithmetic: 70.9 us -> none  [the longest x15 32.6 us: orthonormal(): chol_lower = jnp.linalg.cholesky(gram * inv_rows)]
    dot_general x23 -> x0, matrix products: 70.3 us -> none  [the longest x4 22.8 us: tile_product(): jnp.einsum('mkab,mkbc->mac', tile_part, gathered, preferred_element_type=...]
    ppermute x8 -> x0, starting transfers between devices: 23.6 us -> none  [the longest x4 15.6 us: with_halo(): after = lax.ppermute(initial, axis, down)]
    scatter x7 -> x0, local copies, waits for them, and re-layouts: 13.9 us -> none  [the longest x4 8.15 us: on_device(): hessenberg = hessenberg.at[:(number + 1) * block_width, number * block_wi...]
  transfers between devices with their start and end apart: 9 -> 0, of which waited for: 3 -> 0; matrix products, arithmetic and copies ran while one was open for 3% -> 0% of each run, Pallas kernels for 0% -> 0%
where the time goes in v1:
time: 92.6 us; the launch traced here: 91.6 us
  Pallas kernels  85.8 us (93%)
  local copies, waits for them, and re-layouts  5.04 us (5%)
    pallas_call x1, Pallas kernels, on_device(): pl.pallas_call(functools.partial(krylov_kernel, nr, nw), out_shape=(jax.S...  66.8 us
    pallas_call x1, Pallas kernels, on_device(): pl.pallas_call(functools.partial(finish_kernel, 1.0 / (rows * nr * nw)),...  19 us
    unnamed x8, local copies, waits for them, and re-layouts  5.04 us

profile of v1, /device:TPU:8, one launch (start us, length us, event | category | flops | bytes accessed | tf_op | source)
XLA Modules:
  0.0 91.6 jit_solution(3351171589067091325)
XLA Ops:
  0.6 0.0 copy-start
  0.6 2.5 %copy-done = bf16[32,5,128,128]{3,2,1,0:T(8,128)(2,1)S(1)} copy-done((bf16[32,5,128,128]{3,2,1,0:T(8,128)(2,1)S(1)}, bf16[32,5,128,128]{3,2,1,0:T(8,128)(2,1)}, u32[]{:S(2)}) %copy-start) | copy-done | bytes 5242904
  3.1 0.0 copy-start.1
  3.1 1.2 %copy-done.1 = f32[4096,64]{0,1:T(8,128)S(1)} copy-done((f32[4096,64]{0,1:T(8,128)S(1)}, f32[4096,64]{0,1:T(8,128)}, u32[]{:S(2)}) %copy-start.1) | copy-done | bytes 1048600
  4.3 0.0 copy-start.2
  4.3 0.7 copy-done.2
  5.0 0.0 copy-start.3
  5.0 0.7 copy-done.3
  5.7 66.8 %shard_map.59 = (f32[640,128]{1,0:T(8,128)S(1)}, bf16[5,32,128,128]{3,2,1,0:T(8,128)(2,1)S(1)}) custom-call(s32[5,32]{1,0:T(8,128)S(1)} %bitcast.4, s32[32]{0:T(128)S(1)} %copy-done.3, bf16[32,5,128,128]{3,2,1,0:T(8,128)(2,1)S(1)} %copy-done, f32[64,4096]{1,0:T(8,128)S(1)} %bitcast.3), custom_call_target="tpu_custom_call" | custom-call | tf_op jit(solution)/shard_map/pallas_call | solution.py:467
  72.5 19.0 %shard_map.60 = (f32[64,4096]{1,0:T(8,128)}, f32[320,256]{1,0:T(8,128)}) custom-call(f32[640,128]{1,0:T(8,128)S(1)} %get-tuple-element.6.s_ref, bf16[5,32,128,128]{3,2,1,0:T(8,128)(2,1)S(1)} %get-tuple-element.7.z_hbm), custom_call_target="tpu_custom_call" | custom-call | tf_op jit(solution)/shard_map/pallas_call | solution.py:498
Async XLA Ops:
  0.6 2.5 %copy-start = (bf16[32,5,128,128]{3,2,1,0:T(8,128)(2,1)S(1)}, bf16[32,5,128,128]{3,2,1,0:T(8,128)(2,1)}, u32[]{:S(2)}) copy-start(bf16[32,5,128,128]{3,2,1,0:T(8,128)(2,1)} %tiles.1) | copy-start | bytes 15728644
  3.1 1.2 %copy-start.1 = (f32[4096,64]{0,1:T(8,128)S(1)}, f32[4096,64]{0,1:T(8,128)}, u32[]{:S(2)}) copy-start(f32[4096,64]{0,1:T(8,128)} %param.7) | copy-start | bytes 3145732
  4.3 0.7 copy-start.2
  5.0 0.7 copy-start.3

commit v2 on v1

v2 whole, which is shorter than its diff:
```python
import functools

import jax
import jax.numpy as jnp
from jax import lax
from jax.experimental import pallas as pl
from jax.experimental.pallas import tpu as pltpu
from jax.sharding import PartitionSpec as P

REACH = 2
STEPS = 4
NBLK = STEPS + 1
SHIFTS = (0.0, 0.5, 1.0, 0.25)
F32 = jnp.float32
BF16 = jnp.bfloat16
MESH = pl.DeviceIdType.MESH
HIGHEST = lax.Precision.HIGHEST
NT = (((1,), (1,)), ((), ()))
TN = (((0,), (0,)), ((), ()))
NN = (((1,), (0,)), ((), ()))
BATCHES = ((0, 256), (256, 128), (384, 256))
GRAM_ROWS = 640


def batch_of(j):
    return max(j - 2, 0)


def place(i, j):
    t = j * (j + 1) // 2 + i if j < 3 else i
    return BATCHES[batch_of(j)][0] + (t // 2) * 64, t % 2


def split(x):
    hi = x.astype(BF16)
    lo = (x - hi.astype(F32)).astype(BF16)
    return jnp.concatenate([hi, lo], axis=0)


def mm(a, b, dims=NN):
    return lax.dot_general(a, b, dims, precision=HIGHEST, preferred_element_type=F32)


def gram_block(ref, scale, i, j, first=0):
    row, odd = place(i, j)
    x = ref[row - first : row - first + 64]
    if odd:
        x = pltpu.roll(x, 64, 1)
    return x[:, :64] * scale


def factor(block):
    size = block.shape[0]
    eye = (
        lax.broadcasted_iota(jnp.int32, (size, size), 0)
        == lax.broadcasted_iota(jnp.int32, (size, size), 1)
    ).astype(F32)
    cur = jnp.concatenate([block, eye], axis=1)
    done = []
    for kb in range(size // 8):
        n = size - 8 * kb
        rid = lax.broadcasted_iota(jnp.int32, (n, 128), 0)
        cols = [
            jnp.broadcast_to(cur[:, 8 * kb + p : 8 * kb + p + 1], (n, 128)) for p in range(8)
        ]
        scale = jnp.zeros((8, 128), F32)
        for p in range(8):
            pivot = cols[p][p : p + 1]
            inv = 1.0 / pivot
            scale = jnp.where(rid[:8] == p, lax.rsqrt(pivot), scale)
            mult = jnp.where(rid > p, cols[p] * inv, 0.0)
            cur = cur - mult * cur[p : p + 1]
            for q in range(p + 1, 8):
                cols[q] = cols[q] - mult * cols[q][p : p + 1]
        done.append(cur[:8] * scale)
        cur = cur[8:]
    full = jnp.concatenate(done, axis=0)
    upper = lax.broadcasted_iota(jnp.int32, (size, size), 0) <= lax.broadcasted_iota(
        jnp.int32, (size, size), 1
    )
    r = jnp.where(upper, full[:, :size], 0.0)
    m = pltpu.roll(full, size, 1)[:, :size]
    return r, m


def krylov_kernel(
    nr, nw, scale, nbr_hbm, cnt_hbm, tiles, start, s_out, inv_out, h_out, z_out,
    nbr, cnt, tl, x0, v0, v1, v2, v3, v4, ones, irs, hb, acc, gb, land1, part, land2, gs, bm,
    in_sem, z_sem, hs, hr, s1, r1, s2, r2, s3, r3,
):
    vb = (v0, v1, v2, v3, v4)
    mil = tl.shape[0]
    slots = tl.shape[1]
    zero_at = mil + 2 * REACH
    n = nr * nw
    me_r = lax.axis_index("region")
    me_w = lax.axis_index("within")
    me = me_r * nw + me_w
    base = me * mil
    right = lax.rem(me + 1, n)
    left = lax.rem(me + n - 1, n)
    right_id = (right // nw, lax.rem(right, nw))
    left_id = (left // nw, lax.rem(left, nw))

    start_copy = pltpu.make_async_copy(start, x0, in_sem.at[0])
    start_copy.start()
    index_copies = (
        pltpu.make_async_copy(nbr_hbm, nbr, in_sem.at[5]),
        pltpu.make_async_copy(cnt_hbm, cnt, in_sem.at[6]),
    )
    for cp in index_copies:
        cp.start()
    part_mil = mil // 4
    tile_copies = []
    for c in range(4):
        cp = pltpu.make_async_copy(
            tiles.at[pl.ds(c * part_mil, part_mil)],
            tl.at[pl.ds(c * part_mil, part_mil)],
            in_sem.at[1 + c],
        )
        cp.start()
        tile_copies.append(cp)

    barrier = pltpu.get_barrier_semaphore()
    for o in range(1, nr):
        pl.semaphore_signal(
            barrier, inc=1, device_id=(lax.rem(me_r + o, nr), me_w), device_id_type=MESH
        )
    for o in range(1, nw):
        pl.semaphore_signal(
            barrier, inc=1, device_id=(me_r, lax.rem(me_w + o, nw)), device_id_type=MESH
        )
    pl.semaphore_signal(barrier, inc=1, device_id=right_id, device_id_type=MESH)
    pl.semaphore_signal(barrier, inc=1, device_id=left_id, device_id_type=MESH)

    for j in range(STEPS):
        vb[j][zero_at] = jnp.zeros((128, 128), BF16)
    ones[0] = jnp.ones((16, 128), BF16)
    ones[1] = jnp.zeros((16, 128), BF16)
    for b in (0, 2):
        first, total = BATCHES[b]
        gb[first + total - 64 : first + total] = jnp.zeros((64, 128), F32)
    inv_out[...] = jnp.zeros(inv_out.shape, F32)
    bm[...] = jnp.zeros(bm.shape, F32)

    start_copy.wait()

    def load_start(m):
        lanes = pl.ds(pl.multiple_of(m * 128, 128), 128)
        vb[0][m + REACH] = split(x0[:, lanes])

    edge = list(range(REACH)) + list(range(mil - REACH, mil))
    for m in edge:
        load_start(m)
    pl.semaphore_wait(barrier, nr + nw)

    def halo(j):
        return (
            pltpu.make_async_remote_copy(
                src_ref=vb[j].at[pl.ds(mil, REACH)], dst_ref=hb.at[j, 0],
                send_sem=hs.at[j, 0], recv_sem=hr.at[j, 0],
                device_id=right_id, device_id_type=MESH,
            ),
            pltpu.make_async_remote_copy(
                src_ref=vb[j].at[pl.ds(REACH, REACH)], dst_ref=hb.at[j, 1],
                send_sem=hs.at[j, 1], recv_sem=hr.at[j, 1],
                device_id=left_id, device_id_type=MESH,
            ),
        )

    def start_all(copies):
        for cp in copies:
            cp.start()

    def apply_one(j, m):
        vs, ts = [], []
        for k in range(slots):
            live = k < cnt[m]
            at = jnp.where(live, nbr[k, m] - base + REACH, zero_at)
            v = vb[j][at]
            if j == 0:
                v = jnp.concatenate([v, ones[jnp.where(live, 0, 1)]], axis=0)
            vs.append(v)
            ts.append(tl[m, k])
        prod = lax.dot_general(
            jnp.concatenate(vs, axis=1), jnp.concatenate(ts, axis=1), NT,
            preferred_element_type=F32,
        )
        if j == 0:
            inv = 1.0 / prod[128:136]
            irs[m] = inv
        else:
            inv = irs[m]
        w = (prod[:64] + prod[64:128]) * inv[0:1]
        if SHIFTS[j] != 0.0:
            own = vb[j][m + REACH].astype(F32)
            w = w - SHIFTS[j] * (own[:64] + own[64:])
        vb[j + 1][m + REACH] = split(w)

    group = mil // 2

    def gram(j):
        rows = (j + 1) * 128
        for c in range(mil // group):
            stack = [
                jnp.concatenate([vb[i][REACH + c * group + q] for q in range(group)], axis=1)
                for i in range(j + 1)
            ]
            prod = lax.dot_general(
                jnp.concatenate(stack, axis=0), stack[j], NT, preferred_element_type=F32
            )
            if c == 0:
                acc[:rows] = prod
            else:
                acc[:rows] += prod
        lane = lax.broadcasted_iota(jnp.int32, (64, 128), 1)
        for i in range(j + 1):
            blk = acc[i * 128 : i * 128 + 64] + acc[i * 128 + 64 : i * 128 + 128]
            blk = blk + pltpu.roll(blk, 64, 1)
            row, odd = place(i, j)
            if odd:
                gb[row : row + 64] = jnp.where(lane < 64, gb[row : row + 64], blk)
            else:
                gb[row : row + 64] = blk

    def rows_of(b, c):
        first, total = BATCHES[b]
        size = total // nr
        return pl.ds(pl.multiple_of(first + c * size, 8), size)

    def stage1(b):
        size = BATCHES[b][1] // nr
        out = []
        for o in range(1, nr):
            to = lax.rem(me_r + o, nr)
            out.append(
                pltpu.make_async_remote_copy(
                    src_ref=gb.at[rows_of(b, to)],
                    dst_ref=land1.at[b, o - 1, pl.ds(0, size)],
                    send_sem=s1.at[b, o - 1], recv_sem=r1.at[b, o - 1],
                    device_id=(to, me_w), device_id_type=MESH,
                )
            )
        return out

    def sum1(b):
        size = BATCHES[b][1] // nr
        total = gb[rows_of(b, me_r)]
        for o in range(1, nr):
            total = total + land1[b, o - 1, 0:size]
        part[b, 0:size] = total
        land2[b, me_w, 0:size] = total

    def stage2(b):
        size = BATCHES[b][1] // nr
        out = []
        for o in range(1, nw):
            to = lax.rem(me_w + o, nw)
            out.append(
                pltpu.make_async_remote_copy(
                    src_ref=part.at[b, pl.ds(0, size)],
                    dst_ref=land2.at[b, me_w, pl.ds(0, size)],
                    send_sem=s2.at[b, o - 1], recv_sem=r2.at[b, o - 1],
                    device_id=(me_r, to), device_id_type=MESH,
                )
            )
        return out

    def wait2(b):
        size = BATCHES[b][1] // nr
        for o in range(1, nw):
            frm = lax.rem(me_w + nw - o, nw)
            pltpu.make_async_remote_copy(
                src_ref=part.at[b, pl.ds(0, size)],
                dst_ref=land2.at[b, frm, pl.ds(0, size)],
                send_sem=s2.at[b, o - 1], recv_sem=r2.at[b, o - 1],
                device_id=(me_r, frm), device_id_type=MESH,
            ).wait_recv()

    def sum2(b):
        size = BATCHES[b][1] // nr
        total = land2[b, 0, 0:size]
        for i in range(1, nw):
            total = total + land2[b, i, 0:size]
        gs[rows_of(b, me_r)] = total

    def stage3(b):
        out = []
        for o in range(1, nr):
            to = lax.rem(me_r + o, nr)
            out.append(
                pltpu.make_async_remote_copy(
                    src_ref=gs.at[rows_of(b, me_r)],
                    dst_ref=gs.at[rows_of(b, me_r)],
                    send_sem=s3.at[b, o - 1], recv_sem=r3.at[b, o - 1],
                    device_id=(to, me_w), device_id_type=MESH,
                )
            )
        return out

    def wait3(b):
        for o in range(1, nr):
            frm = lax.rem(me_r + nr - o, nr)
            pltpu.make_async_remote_copy(
                src_ref=gs.at[rows_of(b, frm)],
                dst_ref=gs.at[rows_of(b, frm)],
                send_sem=s3.at[b, o - 1], recv_sem=r3.at[b, o - 1],
                device_id=(frm, me_w), device_id_type=MESH,
            ).wait_recv()

    def wait_sent(copies):
        for cp in copies:
            cp.wait_send()

    def wait_got(copies):
        for cp in copies:
            cp.wait_recv()

    def interior(fn, lo=REACH, hi=mil - REACH):
        def body(m, carry):
            fn(m)
            return carry

        lax.fori_loop(lo, hi, body, 0, unroll=14)

    def chain(j):
        n = 64 * j
        blocks = [gram_block(gs, scale, i, j) for i in range(j + 1)]
        schur = blocks[j]
        if j:
            known = inv_out[0:n, 0:n]
            above = mm(known, jnp.concatenate(blocks[:j], axis=0))
            schur = schur - mm(above, above, TN)
        r, m = factor(schur)
        col = r
        if j:
            inv_out[n : n + 64, 0:n] = -mm(m, mm(above, known, TN))
            col = jnp.concatenate([above, r], axis=0)
            bm[0 : n + 64, n - 64 : n] += col
        inv_out[n : n + 64, n : n + 64] = m
        bm[0 : n + 64, n : n + 64] = SHIFTS[j] * col

    halos = [halo(j) for j in range(STEPS)]
    z_copies = [
        pltpu.make_async_copy(vb[j].at[pl.ds(REACH, mil)], z_out.at[j], z_sem.at[j])
        for j in range(NBLK)
    ]
    first = [stage1(b) for b in range(3)]
    second = [stage2(b) for b in range(3)]
    third = [stage3(b) for b in range(3)]

    def forward1(b):
        wait_got(first[b])
        sum1(b)
        start_all(second[b])

    def forward2(b):
        wait2(b)
        sum2(b)
        start_all(third[b])

    start_all(halos[0])
    interior(load_start)
    middle = mil // 2
    for j in range(STEPS):
        z_copies[j].start()
        gram(j)
        if j == 0:
            for cp in tile_copies:
                cp.wait()
            for cp in index_copies:
                cp.wait()
        step = functools.partial(apply_one, j)
        if j >= 2:
            start_all(first[j - 2])
        if j == STEPS - 1:
            interior(step, REACH, middle)
            forward1(0)
            interior(step, middle, mil - REACH)
        else:
            interior(step)
        wait_got(halos[j])
        vb[j][0:REACH] = hb[j, 0]
        vb[j][mil + REACH : mil + 2 * REACH] = hb[j, 1]
        for m in edge:
            apply_one(j, m)
        if j + 1 < STEPS:
            start_all(halos[j + 1])
    z_copies[STEPS].start()
    gram(STEPS)
    start_all(first[2])
    forward1(1)
    forward2(0)
    for j in range(STEPS):
        wait_sent(halos[j])
    forward1(2)
    forward2(1)
    wait3(0)
    chain(0)
    chain(1)
    forward2(2)
    chain(2)
    wait3(1)
    chain(3)
    h_out[...] = mm(bm[...], inv_out[...], NT)
    for b in range(3):
        wait_sent(first[b])
        wait_sent(second[b])
    wait_sent(third[0])
    wait_sent(third[1])
    for cp in z_copies:
        cp.wait()
    wait3(2)
    s_out[...] = gs[BATCHES[2][0] :]
    wait_sent(third[2])


def finish_kernel(scale, s_ref, inv_ref, hp_ref, z_hbm, q_ref, h_ref, zb, sems):
    mil = zb.shape[1]
    copies = [pltpu.make_async_copy(z_hbm.at[k], zb.at[k], sems.at[k]) for k in range(NBLK)]
    for cp in copies:
        cp.start()

    n = 64 * STEPS
    blocks = [gram_block(s_ref, scale, i, STEPS, BATCHES[2][0]) for i in range(NBLK)]
    known = inv_ref[...]
    above = mm(known, jnp.concatenate(blocks[:STEPS], axis=0))
    r, m = factor(blocks[STEPS] - mm(above, above, TN))
    row = -mm(m, mm(above, known, TN))
    coef = []
    for k in range(NBLK):
        c = m
        if k < STEPS:
            c = row[:, 128 * (k // 2) : 128 * (k // 2) + 128]
            if k % 2:
                c = pltpu.roll(c, 64, 1)
            c = c[:, :64]
        hi = c.astype(BF16)
        lo = (c - hi.astype(F32)).astype(BF16)
        coef.append(
            jnp.concatenate(
                [jnp.concatenate([hi, hi], axis=1), jnp.concatenate([lo, lo], axis=1)], axis=0
            )
        )
    coef = jnp.concatenate(coef, axis=1)

    corner = pltpu.roll(inv_ref[n - 64 : n, n - 128 : n], 64, 1)[:, :64]
    h_ref[:, 0 : n - 64] = hp_ref[:, 0 : n - 64]
    h_ref[:, n - 64 : n] = hp_ref[:, n - 64 : n] + mm(
        jnp.concatenate([above, r], axis=0), corner, NT
    )

    for cp in copies:
        cp.wait()

    def body(g, carry):
        right = jnp.concatenate(
            [jnp.concatenate([zb[k, 2 * g], zb[k, 2 * g + 1]], axis=1) for k in range(NBLK)],
            axis=0,
        )
        prod = lax.dot_general(coef, right, NN, preferred_element_type=F32)
        q_ref[:, pl.ds(pl.multiple_of(g * 256, 256), 256)] = prod[:64] + prod[64:]
        return carry

    lax.fori_loop(0, mil // 2, body, 0, unroll=8)


def in_hbm(*arrays):
    return [pltpu.with_memory_space_constraint(a, pltpu.HBM) for a in arrays]


def on_device(nr, nw, kernel_tiles, neighbours, tile_counts, start_block):
    mil, slots, states = kernel_tiles.shape[:3]
    width = start_block.shape[1]
    rows = mil * states
    scale = 1.0 / (rows * nr * nw)
    vmem = pl.BlockSpec(memory_space=pltpu.VMEM)
    hbm = pl.BlockSpec(memory_space=pltpu.HBM)
    size = 256 // nr
    square = STEPS * width
    dma = pltpu.SemaphoreType.DMA
    vec = pltpu.VMEM((mil + 2 * REACH + 1, 2 * width, states), BF16)
    packed, inv, part, z = pl.pallas_call(
        functools.partial(krylov_kernel, nr, nw, scale),
        out_shape=(
            jax.ShapeDtypeStruct((256, 128), F32),
            jax.ShapeDtypeStruct((square, square), F32),
            jax.ShapeDtypeStruct((NBLK * width, square), F32),
            jax.ShapeDtypeStruct((NBLK, mil, 2 * width, states), BF16),
        ),
        in_specs=[hbm, hbm, hbm, hbm],
        out_specs=(vmem, vmem, vmem, hbm),
        scratch_shapes=[
            pltpu.SMEM((slots, mil), jnp.int32),
            pltpu.SMEM((mil,), jnp.int32),
            pltpu.VMEM((mil, slots, states, states), BF16),
            pltpu.VMEM((width, rows), F32),
            vec, vec, vec, vec, vec,
            pltpu.VMEM((2, 16, 128), BF16),
            pltpu.VMEM((mil, 8, 128), F32),
            pltpu.VMEM((STEPS, 2, REACH, 2 * width, states), BF16),
            pltpu.VMEM((NBLK * 128, 128), F32),
            pltpu.VMEM((GRAM_ROWS, 128), F32),
            pltpu.VMEM((3, nr, size, 128), F32),
            pltpu.VMEM((3, size, 128), F32),
            pltpu.VMEM((3, nw, size, 128), F32),
            pltpu.VMEM((GRAM_ROWS, 128), F32),
            pltpu.VMEM((NBLK * width, square), F32),
            dma((7,)), dma((NBLK,)),
            dma((STEPS, 2)), dma((STEPS, 2)),
            dma((3, nr)), dma((3, nr)),
            dma((3, nw)), dma((3, nw)),
            dma((3, nr)), dma((3, nr)),
        ],
        compiler_params=pltpu.CompilerParams(
            collective_id=0, has_side_effects=True, vmem_limit_bytes=40 * 1024 * 1024
        ),
    )(*in_hbm(neighbours.T, tile_counts, kernel_tiles, start_block.T))
    last, hess = pl.pallas_call(
        functools.partial(finish_kernel, scale),
        out_shape=(
            jax.ShapeDtypeStruct((width, rows), F32),
            jax.ShapeDtypeStruct((NBLK * width, square), F32),
        ),
        in_specs=[vmem, vmem, vmem, hbm],
        out_specs=(vmem, vmem),
        scratch_shapes=[
            pltpu.VMEM((NBLK, mil, 2 * width, states), BF16),
            dma((NBLK,)),
        ],
        compiler_params=pltpu.CompilerParams(vmem_limit_bytes=40 * 1024 * 1024),
    )(packed, inv, part, z)
    return last.T, hess


def solution(mesh):
    nr, nw = mesh.shape["region"], mesh.shape["within"]
    return jax.shard_map(
        functools.partial(on_device, nr, nw),
        mesh=mesh,
        in_specs=(
            P(("region", "within"), None, None, None),
            P(("region", "within"), None),
            P(("region", "within")),
            P(("region", "within"), None),
        ),
        out_specs=(P(("region", "within"), None), P()),
        check_vma=False,
    )
```

time: 92.6 us -> 61.9 us (0.67)
  Pallas kernels: 85.8 us -> 61 us
  local copies, waits for them, and re-layouts: 5.04 us -> 0 us
    pallas_call x2, Pallas kernels: 85.8 us -> 61 us  [the longest x1 55.4 us: on_device(): pl.pallas_call(functools.partial(krylov_kernel, nr, nw, scale), out_shape...]
    unnamed x8 -> x0, local copies, waits for them, and re-layouts: 5.04 us -> none
where the time goes in v2:
time: 61.9 us; the launch traced here: 61.8 us
  Pallas kernels  61 us (99%)
  between operations  0.8 us (1%)
    pallas_call x1, Pallas kernels, on_device(): pl.pallas_call(functools.partial(krylov_kernel, nr, nw, scale), out_shape...  55.4 us
    pallas_call x1, Pallas kernels, on_device(): pl.pallas_call(functools.partial(finish_kernel, scale), out_shape=(jax.Sh...  5.64 us

profile of v2, /device:TPU:8, one launch (start us, length us, event | category | flops | bytes accessed | tf_op | source)
XLA Modules:
  0.0 61.8 jit_solution(9432435631123916240)
XLA Ops:
  0.6 55.4 %shard_map.59 = (f32[256,128]{1,0:T(8,128)S(1)}, f32[256,256]{1,0:T(8,128)S(1)}, f32[320,256]{1,0:T(8,128)S(1)}, bf16[5,32,128,128]{3,2,1,0:T(8,128)(2,1)S(1)}) custom-call(s32[5,32]{1,0:T(8,128)} %bitcast.4, s32[32]{0:T(128)} %cnt_hbm.1, bf16[32,5,128,128]{3,2,1,0:T(8,128)(2,1)} %tiles.1, f32[64,4096]{1,0:T(8,128)} %bitcast.3), custom_call_target="tpu_custom_call" | custom-call | tf_op jit(solution)/shard_map/pallas_call | solution.py:483
  56.0 5.6 %shard_map.60 = (f32[64,4096]{1,0:T(8,128)}, f32[320,256]{1,0:T(8,128)}) custom-call(f32[256,128]{1,0:T(8,128)S(1)} %get-tuple-element.8.s_ref, f32[256,256]{1,0:T(8,128)S(1)} %get-tuple-element.9.inv_ref, f32[320,256]{1,0:T(8,128)S(1)} %get-tuple-element.10.hp_ref, bf16[5,32,128,128]{3,2,1,0:T(8,128)(2,1)S(1)} %get-tuple-element.11.z_hbm), custom_call_target="tpu_custom_call" | custom-call | tf_op jit(solution)/shard_map/pallas_call | solution.py:519

commit v3 on v2

--- a/solution.py
+++ b/solution.py
@@ -21,14 +21,9 @@
 BATCHES = ((0, 256), (256, 128), (384, 256))
 GRAM_ROWS = 640
 
-
-def batch_of(j):
-    return max(j - 2, 0)
-
-
 def place(i, j):
-    t = j * (j + 1) // 2 + i if j < 3 else i
-    return BATCHES[batch_of(j)][0] + (t // 2) * 64, t % 2
+    t = i + (j * (j + 1) // 2 if j < 3 else 0)
+    return BATCHES[max(j - 2, 0)][0] + (t // 2) * 64, t % 2
 
 
 def split(x):
@@ -64,14 +59,23 @@
             jnp.broadcast_to(cur[:, 8 * kb + p : 8 * kb + p + 1], (n, 128)) for p in range(8)
         ]
         scale = jnp.zeros((8, 128), F32)
-        for p in range(8):
-            pivot = cols[p][p : p + 1]
-            inv = 1.0 / pivot
-            scale = jnp.where(rid[:8] == p, lax.rsqrt(pivot), scale)
-            mult = jnp.where(rid > p, cols[p] * inv, 0.0)
-            cur = cur - mult * cur[p : p + 1]
-            for q in range(p + 1, 8):
-                cols[q] = cols[q] - mult * cols[q][p : p + 1]
+        for p in range(0, 8, 2):
+            a, b, c = cols[p][p : p + 1], cols[p][p + 1 : p + 2], cols[p + 1][p + 1 : p + 2]
+            det = a * c - b * b
+            inv_a = 1.0 / a
+            inv_c = a * (1.0 / det)
+            ratio = b * inv_a
+            scale = jnp.where(rid[:8] == p, lax.rsqrt(a), scale)
+            scale = jnp.where(rid[:8] == p + 1, lax.rsqrt(det * inv_a), scale)
+            mult0 = jnp.where(rid > p, cols[p] * inv_a, 0.0)
+            mult1 = jnp.where(rid > p + 1, (cols[p + 1] - mult0 * b) * inv_c, 0.0)
+            row0 = cur[p : p + 1]
+            row1 = cur[p + 1 : p + 2] - ratio * row0
+            cur = cur - mult0 * row0 - mult1 * row1
+            for q in range(p + 2, 8):
+                q0 = cols[q][p : p + 1]
+                q1 = cols[q][p + 1 : p + 2] - ratio * q0
+                cols[q] = cols[q] - mult0 * q0 - mult1 * q1
         done.append(cur[:8] * scale)
         cur = cur[8:]
     full = jnp.concatenate(done, axis=0)
@@ -84,12 +88,12 @@
 
 
 def krylov_kernel(
-    nr, nw, scale, nbr_hbm, cnt_hbm, tiles, start, s_out, inv_out, h_out, z_out,
-    nbr, cnt, tl, x0, v0, v1, v2, v3, v4, ones, irs, hb, acc, gb, land1, part, land2, gs, bm,
+    nr, nw, scale, nbr_hbm, cnt_hbm, tiles, start, s_out, inv_out, bm, z_out,
+    nbr, cnt, tl, x0, v0, v1, v2, v3, v4, ones, irs, hb, acc, gb, land1, part, land2, gs,
     in_sem, z_sem, hs, hr, s1, r1, s2, r2, s3, r3,
 ):
     vb = (v0, v1, v2, v3, v4)
-    mil = tl.shape[0]
+    mil = z_out.shape[1]
     slots = tl.shape[1]
     zero_at = mil + 2 * REACH
     n = nr * nw
@@ -101,6 +105,18 @@
     left = lax.rem(me + n - 1, n)
     right_id = (right // nw, lax.rem(right, nw))
     left_id = (left // nw, lax.rem(left, nw))
+
+    barrier = pltpu.get_barrier_semaphore()
+    for o in range(1, nr):
+        pl.semaphore_signal(
+            barrier, inc=1, device_id=(lax.rem(me_r + o, nr), me_w), device_id_type=MESH
+        )
+    for o in range(1, nw):
+        pl.semaphore_signal(
+            barrier, inc=1, device_id=(me_r, lax.rem(me_w + o, nw)), device_id_type=MESH
+        )
+    pl.semaphore_signal(barrier, inc=1, device_id=right_id, device_id_type=MESH)
+    pl.semaphore_signal(barrier, inc=1, device_id=left_id, device_id_type=MESH)
 
     start_copy = pltpu.make_async_copy(start, x0, in_sem.at[0])
     start_copy.start()
@@ -121,25 +137,12 @@
         cp.start()
         tile_copies.append(cp)
 
-    barrier = pltpu.get_barrier_semaphore()
-    for o in range(1, nr):
-        pl.semaphore_signal(
-            barrier, inc=1, device_id=(lax.rem(me_r + o, nr), me_w), device_id_type=MESH
-        )
-    for o in range(1, nw):
-        pl.semaphore_signal(
-            barrier, inc=1, device_id=(me_r, lax.rem(me_w + o, nw)), device_id_type=MESH
-        )
-    pl.semaphore_signal(barrier, inc=1, device_id=right_id, device_id_type=MESH)
-    pl.semaphore_signal(barrier, inc=1, device_id=left_id, device_id_type=MESH)
-
     for j in range(STEPS):
         vb[j][zero_at] = jnp.zeros((128, 128), BF16)
     ones[0] = jnp.ones((16, 128), BF16)
     ones[1] = jnp.zeros((16, 128), BF16)
-    for b in (0, 2):
-        first, total = BATCHES[b]
-        gb[first + total - 64 : first + total] = jnp.zeros((64, 128), F32)
+    for row in (192, GRAM_ROWS - 64):
+        gb[row : row + 64] = jnp.zeros((64, 128), F32)
     inv_out[...] = jnp.zeros(inv_out.shape, F32)
     bm[...] = jnp.zeros(bm.shape, F32)
 
@@ -149,8 +152,7 @@
         lanes = pl.ds(pl.multiple_of(m * 128, 128), 128)
         vb[0][m + REACH] = split(x0[:, lanes])
 
-    edge = list(range(REACH)) + list(range(mil - REACH, mil))
-    for m in edge:
+    for m in list(range(REACH)) + list(range(mil - REACH, mil)):
         load_start(m)
     pl.semaphore_wait(barrier, nr + nw)
 
@@ -173,7 +175,7 @@
             cp.start()
 
     def apply_one(j, m):
-        vs, ts = [], []
+        vs, tiles_m = [], []
         for k in range(slots):
             live = k < cnt[m]
             at = jnp.where(live, nbr[k, m] - base + REACH, zero_at)
@@ -181,9 +183,9 @@
             if j == 0:
                 v = jnp.concatenate([v, ones[jnp.where(live, 0, 1)]], axis=0)
             vs.append(v)
-            ts.append(tl[m, k])
+            tiles_m.append(tl[m, k])
         prod = lax.dot_general(
-            jnp.concatenate(vs, axis=1), jnp.concatenate(ts, axis=1), NT,
+            jnp.concatenate(vs, axis=1), jnp.concatenate(tiles_m, axis=1), NT,
             preferred_element_type=F32,
         )
         if j == 0:
@@ -197,22 +199,25 @@
             w = w - SHIFTS[j] * (own[:64] + own[64:])
         vb[j + 1][m + REACH] = split(w)
 
-    group = mil // 2
+    def accumulate(j, milestones, fresh):
+        rows = (j + 1) * 128
+        stack = [
+            jnp.concatenate([vb[i][REACH + m] for m in milestones], axis=1) for i in range(j + 1)
+        ]
+        prod = lax.dot_general(
+            jnp.concatenate(stack, axis=0), stack[j], NT, preferred_element_type=F32
+        )
+        if fresh:
+            acc[:rows] = prod
+        else:
+            acc[:rows] += prod
 
     def gram(j):
-        rows = (j + 1) * 128
-        for c in range(mil // group):
-            stack = [
-                jnp.concatenate([vb[i][REACH + c * group + q] for q in range(group)], axis=1)
-                for i in range(j + 1)
-            ]
-            prod = lax.dot_general(
-                jnp.concatenate(stack, axis=0), stack[j], NT, preferred_element_type=F32
-            )
-            if c == 0:
-                acc[:rows] = prod
-            else:
-                acc[:rows] += prod
+        accumulate(j, range(mil // 2), True)
+        accumulate(j, range(mil // 2, mil), False)
+        fold(j)
+
+    def fold(j):
         lane = lax.broadcasted_iota(jnp.int32, (64, 128), 1)
         for i in range(j + 1):
             blk = acc[i * 128 : i * 128 + 64] + acc[i * 128 + 64 : i * 128 + 128]
@@ -316,12 +321,12 @@
         for cp in copies:
             cp.wait_recv()
 
-    def interior(fn, lo=REACH, hi=mil - REACH):
+    def interior(fn, lo, hi):
         def body(m, carry):
             fn(m)
             return carry
 
-        lax.fori_loop(lo, hi, body, 0, unroll=14)
+        lax.fori_loop(lo, hi, body, 0, unroll=(hi - lo) // 2)
 
     def chain(j):
         n = 64 * j
@@ -359,40 +364,70 @@
         sum2(b)
         start_all(third[b])
 
-    start_all(halos[0])
-    interior(load_start)
-    middle = mil // 2
-    for j in range(STEPS):
-        z_copies[j].start()
-        gram(j)
-        if j == 0:
-            for cp in tile_copies:
-                cp.wait()
-            for cp in index_copies:
-                cp.wait()
-        step = functools.partial(apply_one, j)
-        if j >= 2:
-            start_all(first[j - 2])
-        if j == STEPS - 1:
-            interior(step, REACH, middle)
-            forward1(0)
-            interior(step, middle, mil - REACH)
-        else:
-            interior(step)
+    def receive(j):
         wait_got(halos[j])
         vb[j][0:REACH] = hb[j, 0]
         vb[j][mil + REACH : mil + 2 * REACH] = hb[j, 1]
-        for m in edge:
+
+    def between(j, lo, hi):
+        for m in list(range(lo, hi)) + list(range(mil - hi, mil - lo)):
             apply_one(j, m)
-        if j + 1 < STEPS:
-            start_all(halos[j + 1])
+
+    def edges(j):
+        between(j, 0, REACH)
+
+    def inner(j, w):
+        interior(functools.partial(apply_one, j), w, mil - w)
+
+    def get_tiles():
+        for cp in tile_copies:
+            cp.wait()
+        for cp in index_copies:
+            cp.wait()
+
+    def publish(j):
+        z_copies[j].start()
+        gram(j)
+        if j > 1:
+            start_all(first[j - 2])
+
+    middle = mil // 2
+    start_all(halos[0])
+    interior(load_start, REACH, mil - REACH)
+    publish(0)
+    get_tiles()
+    inner(0, REACH)
+    inner(1, 2 * REACH)
+    receive(0)
+    edges(0)
+    start_all(halos[1])
+    between(1, REACH, 2 * REACH)
+    publish(1)
+    inner(2, 2 * REACH)
+    receive(1)
+    edges(1)
+    start_all(halos[2])
+    between(2, REACH, 2 * REACH)
+    publish(2)
+    inner(3, 2 * REACH)
+    receive(2)
+    edges(2)
+    start_all(halos[3])
+    publish(3)
+    forward1(0)
+    between(3, REACH, 2 * REACH)
+    accumulate(STEPS, range(REACH, middle), True)
+    accumulate(STEPS, range(middle, mil - REACH), False)
+    receive(3)
+    edges(3)
     z_copies[STEPS].start()
-    gram(STEPS)
+    accumulate(STEPS, list(range(REACH)) + list(range(mil - REACH, mil)), False)
+    fold(STEPS)
     start_all(first[2])
+    for j in range(STEPS):
+        wait_sent(halos[j])
     forward1(1)
     forward2(0)
-    for j in range(STEPS):
-        wait_sent(halos[j])
     forward1(2)
     forward2(1)
     wait3(0)
@@ -402,7 +437,6 @@
     chain(2)
     wait3(1)
     chain(3)
-    h_out[...] = mm(bm[...], inv_out[...], NT)
     for b in range(3):
         wait_sent(first[b])
         wait_sent(second[b])
@@ -415,7 +449,7 @@
     wait_sent(third[2])
 
 
-def finish_kernel(scale, s_ref, inv_ref, hp_ref, z_hbm, q_ref, h_ref, zb, sems):
+def finish_kernel(scale, s_ref, inv_ref, bm_ref, z_hbm, q_ref, h_ref, zb, sems):
     mil = zb.shape[1]
     copies = [pltpu.make_async_copy(z_hbm.at[k], zb.at[k], sems.at[k]) for k in range(NBLK)]
     for cp in copies:
@@ -445,8 +479,9 @@
     coef = jnp.concatenate(coef, axis=1)
 
     corner = pltpu.roll(inv_ref[n - 64 : n, n - 128 : n], 64, 1)[:, :64]
-    h_ref[:, 0 : n - 64] = hp_ref[:, 0 : n - 64]
-    h_ref[:, n - 64 : n] = hp_ref[:, n - 64 : n] + mm(
+    known_h = mm(bm_ref[...], known, NT)
+    h_ref[:, 0 : n - 64] = known_h[:, 0 : n - 64]
+    h_ref[:, n - 64 : n] = known_h[:, n - 64 : n] + mm(
         jnp.concatenate([above, r], axis=0), corner, NT
     )
 
@@ -505,7 +540,6 @@
             pltpu.VMEM((3, size, 128), F32),
             pltpu.VMEM((3, nw, size, 128), F32),
             pltpu.VMEM((GRAM_ROWS, 128), F32),
-            pltpu.VMEM((NBLK * width, square), F32),
             dma((7,)), dma((NBLK,)),
             dma((STEPS, 2)), dma((STEPS, 2)),
             dma((3, nr)), dma((3, nr)),

time: 61.9 us -> 59.4 us (0.960)
  Pallas kernels: 61 us -> 58.5 us
    pallas_call x1, Pallas kernels: 55.4 us -> 52.8 us  [on_device(): pl.pallas_call(functools.partial(krylov_kernel, nr, nw, scale), out_shape...]
where the time goes in v3:
time: 59.4 us; the launch traced here: 59.3 us
  Pallas kernels  58.5 us (98%)
  between operations  0.8 us (1%)
    pallas_call x1, Pallas kernels, on_device(): pl.pallas_call(functools.partial(krylov_kernel, nr, nw, scale), out_shape...  52.8 us
    pallas_call x1, Pallas kernels, on_device(): pl.pallas_call(functools.partial(finish_kernel, scale), out_shape=(jax.Sh...  5.7 us

profile of v3, /device:TPU:8, one launch (start us, length us, event | category | flops | bytes accessed | tf_op | source)
XLA Modules:
  0.0 59.3 jit_solution(17918649273408225972)
XLA Ops:
  0.6 52.8 %shard_map.59 = (f32[256,128]{1,0:T(8,128)S(1)}, f32[256,256]{1,0:T(8,128)S(1)}, f32[320,256]{1,0:T(8,128)S(1)}, bf16[5,32,128,128]{3,2,1,0:T(8,128)(2,1)S(1)}) custom-call(s32[5,32]{1,0:T(8,128)} %bitcast.4, s32[32]{0:T(128)} %cnt_hbm.1, bf16[32,5,128,128]{3,2,1,0:T(8,128)(2,1)} %tiles.1, f32[64,4096]{1,0:T(8,128)} %bitcast.3), custom_call_target="tpu_custom_call" | custom-call | tf_op jit(solution)/shard_map/pallas_call | solution.py:518
  53.4 5.7 %shard_map.60 = (f32[64,4096]{1,0:T(8,128)}, f32[320,256]{1,0:T(8,128)}) custom-call(f32[256,128]{1,0:T(8,128)S(1)} %get-tuple-element.8.s_ref, f32[256,256]{1,0:T(8,128)S(1)} %get-tuple-element.9.inv_ref, f32[320,256]{1,0:T(8,128)S(1)} %get-tuple-element.10.bm_ref, bf16[5,32,128,128]{3,2,1,0:T(8,128)(2,1)S(1)} %get-tuple-element.11.z_hbm), custom_call_target="tpu_custom_call" | custom-call | tf_op jit(solution)/shard_map/pallas_call | solution.py:553

commit v4 on v3

--- a/solution.py
+++ b/solution.py
@@ -449,7 +449,7 @@
     wait_sent(third[2])
 
 
-def finish_kernel(scale, s_ref, inv_ref, bm_ref, z_hbm, q_ref, h_ref, zb, sems):
+def finish_kernel(scale, s_ref, inv_ref, bm_ref, z_hbm, q_hbm, h_ref, zb, q_ref, sems, out_sems):
     mil = zb.shape[1]
     copies = [pltpu.make_async_copy(z_hbm.at[k], zb.at[k], sems.at[k]) for k in range(NBLK)]
     for cp in copies:
@@ -497,7 +497,16 @@
         q_ref[:, pl.ds(pl.multiple_of(g * 256, 256), 256)] = prod[:64] + prod[64:]
         return carry
 
-    lax.fori_loop(0, mil // 2, body, 0, unroll=8)
+    quarter = mil // 8
+    outs = []
+    for c in range(4):
+        lax.fori_loop(c * quarter, (c + 1) * quarter, body, 0, unroll=quarter)
+        lanes = pl.ds(c * quarter * 256, quarter * 256)
+        out = pltpu.make_async_copy(q_ref.at[:, lanes], q_hbm.at[:, lanes], out_sems.at[c])
+        out.start()
+        outs.append(out)
+    for out in outs:
+        out.wait()
 
 
 def in_hbm(*arrays):
@@ -557,10 +566,12 @@
             jax.ShapeDtypeStruct((NBLK * width, square), F32),
         ),
         in_specs=[vmem, vmem, vmem, hbm],
-        out_specs=(vmem, vmem),
+        out_specs=(hbm, vmem),
         scratch_shapes=[
             pltpu.VMEM((NBLK, mil, 2 * width, states), BF16),
+            pltpu.VMEM((width, rows), F32),
             dma((NBLK,)),
+            dma((4,)),
         ],
         compiler_params=pltpu.CompilerParams(vmem_limit_bytes=40 * 1024 * 1024),
     )(packed, inv, part, z)

time: 59.4 us -> 59.6 us (level)
  no operation moved by 1% of the time
where the time goes in v4:
time: 59.6 us
  Pallas kernels  58.8 us (99%)
  between operations  0.8 us (1%)
    pallas_call x1, Pallas kernels, on_device(): pl.pallas_call(functools.partial(krylov_kernel, nr, nw, scale), out_shape...  52.8 us
    pallas_call x1, Pallas kernels, on_device(): pl.pallas_call(functools.partial(finish_kernel, scale), out_shape=(jax.Sh...  5.97 us

profile of v4, /device:TPU:8, one launch (start us, length us, event | category | flops | bytes accessed | tf_op | source)
XLA Modules:
  0.0 59.6 jit_solution(9599279963344321642)
XLA Ops:
  0.6 52.8 %shard_map.59 = (f32[256,128]{1,0:T(8,128)S(1)}, f32[256,256]{1,0:T(8,128)S(1)}, f32[320,256]{1,0:T(8,128)S(1)}, bf16[5,32,128,128]{3,2,1,0:T(8,128)(2,1)S(1)}) custom-call(s32[5,32]{1,0:T(8,128)} %bitcast.4, s32[32]{0:T(128)} %cnt_hbm.1, bf16[32,5,128,128]{3,2,1,0:T(8,128)(2,1)} %tiles.1, f32[64,4096]{1,0:T(8,128)} %bitcast.3), custom_call_target="tpu_custom_call" | custom-call | tf_op jit(solution)/shard_map/pallas_call | solution.py:527
  53.4 6.0 %shard_map.60 = (f32[64,4096]{1,0:T(8,128)}, f32[320,256]{1,0:T(8,128)}) custom-call(f32[256,128]{1,0:T(8,128)S(1)} %get-tuple-element.8.s_ref, f32[256,256]{1,0:T(8,128)S(1)} %get-tuple-element.9.inv_ref, f32[320,256]{1,0:T(8,128)S(1)} %get-tuple-element.10.bm_ref, bf16[5,32,128,128]{3,2,1,0:T(8,128)(2,1)S(1)} %get-tuple-element.11.z_hbm), custom_call_target="tpu_custom_call" | custom-call | tf_op jit(solution)/shard_map/pallas_call | solution.py:562
